TPU v7x, 512 devices: a whole 4x8x8 slice. The times are simulated.
512 devices in a mesh: dp: 16 (over z, core), cell: 32 (over x, y).
Axes of the slice: x: 4, y: 8, z: 8, core: 2. Of those that a mesh axis runs over, the one named last changes fastest.
Arguments:
- configs: int32 [2048, 4], P('dp'), may hold values from 0 to 2047, all different within a row
- pole_fields: bfloat16 [3, 2048, 32768], P(None, 'dp', 'cell'), may hold values from -3 to 3
- misfit: float32 [2048], P('dp'), may hold values from -6 to 6
- data_weight: float32 [2048], P('dp'), may hold values from 0.3 to 3
- conductivity: float32 [32768], P('cell'), may hold values from -6 to 6
- face_weights: float32 [3, 32768], P(None, 'cell'), may hold values from 0.05 to 0.5
Outputs:
- update: float32 [32768], P('cell')
- data_change: float32 [2048], P('dp')
Inputs may be any that keep to these rules, and one draw needn't show every extreme that they name: `configs`: each row names four different poles.
All inputs are finite; a program needn't handle non-finite values.
Results may differ from a plain program's by a relative error of at most 0.0003.
Values may be sent and summed in bfloat16 or wider, within the bound.
A program may use at most 64 MiB of HBM per device.

v0:
```python
import math

import jax
import jax.numpy as jnp
from jax import lax
from jax.sharding import PartitionSpec as P

GY = 32
GZ = 32
ITERS = 3


DAMPING = 0.2


def from_behind(value, axis, steps):
    count = lax.axis_size(axis)
    first, last = (max(0, -steps), min(count, count - steps))
    return lax.ppermute(value, axis, [(source, source + steps) for source in range(first, last)])


def extended(cells, sides, width):
    for axis, dim in sides:
        count = lax.axis_size(axis)
        ends = count - 1
        head = lax.slice_in_dim(cells, 0, width, axis=dim)
        tail = lax.slice_in_dim(cells, cells.shape[dim] - width, cells.shape[dim], axis=dim)
        cells = jnp.concatenate(
            [
                lax.ppermute(tail, axis, [(i, (i + 1) % count) for i in range(ends)]),
                cells,
                lax.ppermute(head, axis, [((i + 1) % count, i) for i in range(ends)]),
            ],
            axis=dim,
        )
    return cells


def per_device(configs, pole_fields, misfit, data_weight, conductivity, face_weights):
    high = lax.Precision.HIGHEST
    row_count = configs.shape[0]
    cell_count = conductivity.shape[0]
    plane_size = GY * GZ
    plane_count = cell_count // plane_size
    data_total = lax.axis_size("dp") * row_count
    fields_part = lax.all_gather(pole_fields, "dp", axis=1, tiled=True)
    pole_count = fields_part.shape[1]
    pole_ids = lax.broadcasted_iota(jnp.int32, (1, pole_count), 1)
    source_signs = (configs[:, 0:1] == pole_ids).astype(jnp.bfloat16) - (
        configs[:, 1:2] == pole_ids
    ).astype(jnp.bfloat16)
    receiver_signs = (configs[:, 2:3] == pole_ids).astype(jnp.bfloat16) - (
        configs[:, 3:4] == pole_ids
    ).astype(jnp.bfloat16)
    source_part = jnp.einsum(
        "dn,knc->kdc", source_signs, fields_part, preferred_element_type=jnp.float32
    )
    receiver_part = jnp.einsum(
        "dn,knc->kdc", receiver_signs, fields_part, preferred_element_type=jnp.float32
    )
    sensitivity = -(
        source_part[0] * receiver_part[0]
        + source_part[1] * receiver_part[1]
        + source_part[2] * receiver_part[2]
    ) / math.sqrt(data_total)
    previous_faces = from_behind(face_weights[0, cell_count - plane_size :], "cell", 1)
    global_plane = lax.axis_index("cell") * plane_count + lax.broadcasted_iota(
        jnp.int32, (plane_count, 1), 0
    )
    plane_mask = (global_plane < lax.axis_size("cell") * plane_count - 1).astype(jnp.float32)
    column = lax.broadcasted_iota(jnp.int32, (1, plane_size - 1), 1)
    column_mask = (column % GZ != GZ - 1).astype(jnp.float32)
    weights_first = jnp.concatenate(
        [
            previous_faces.reshape(1, plane_size),
            face_weights[0].reshape(plane_count, plane_size) * plane_mask,
        ],
        0,
    )
    weights_second = face_weights[1].reshape(plane_count, plane_size)[:, : plane_size - GZ]
    weights_third = (
        face_weights[2].reshape(plane_count, plane_size)[:, : plane_size - 1] * column_mask
    )

    def roughness(vector):
        padded = extended(vector, (("cell", 0),), plane_size)
        planes = padded.reshape(plane_count + 2, plane_size)
        inner = planes[1:-1]
        flux = weights_first * (planes[1:] - planes[:-1])
        result = flux[:-1] - flux[1:]
        flux_second = weights_second * (inner[:, GZ:] - inner[:, :-GZ])
        result = (
            result
            - jnp.pad(flux_second, ((0, 0), (0, GZ)))
            + jnp.pad(flux_second, ((0, 0), (GZ, 0)))
        )
        flux_third = weights_third * (inner[:, 1:] - inner[:, :-1])
        result = (
            result - jnp.pad(flux_third, ((0, 0), (0, 1))) + jnp.pad(flux_third, ((0, 0), (1, 0)))
        )
        return result.reshape(-1)

    def spread(model_term):
        return lax.psum(model_term, "dp")

    def global_sum(values):
        return lax.psum(values, "cell")

    def data_image(whole):
        return lax.psum(jnp.dot(sensitivity, whole, precision=high), "cell")

    gradient = spread(jnp.dot(data_weight * misfit, sensitivity, precision=high)) - roughness(
        conductivity
    )
    update = jnp.zeros_like(gradient)
    residual = gradient
    direction = gradient
    norm_now = global_sum(jnp.sum(residual * residual))
    for iteration in range(ITERS):
        apply_whole = direction
        predicted = data_image(apply_whole)
        apply_model_term = jnp.dot(data_weight * predicted, sensitivity, precision=high)
        image = spread(apply_model_term) + (roughness(apply_whole) + DAMPING * apply_whole)
        step_length = norm_now / global_sum(jnp.sum(direction * image))
        update = update + step_length * direction
        residual = residual - step_length * image
        norm_next = global_sum(jnp.sum(residual * residual))
        direction = residual + norm_next / norm_now * direction
        norm_now = norm_next
    data_change = data_image(update)
    return (update, data_change)


def solution(mesh):
    placed = (P("dp", None), P(None, "dp", "cell"), P("dp"), P("dp"), P("cell"), P(None, "cell"))
    return jax.shard_map(
        per_device, mesh=mesh, in_specs=placed, out_specs=(P("cell"), P("dp")), check_vma=False
    )
```

profile of v0, /device:TPU:8, one launch (start us, length us, event | category | flops | bytes accessed | tf_op | source)
XLA Modules:
  0.0 878.7 jit_solution(221614340284560004)
XLA Ops:
  7.2 0.0 all-gather.2.cloned.1.call-start
  7.2 0.7 all-gather.2.cloned.1.call-update
  7.9 7.7 collective-permute-start.1
  15.6 1.9 collective-permute-start.2
  17.6 0.7 fusion.53
  18.3 1.9 collective-permute-start
  20.2 0.8 fusion.34
  21.1 0.8 fusion.33
  21.9 0.8 slice_bitcast_fusion.3
  22.7 0.0 collective-permute-done.1
  22.7 0.0 collective-permute-done.2
  22.7 0.8 maximum_subtract_fusion
  23.5 0.3 collective-permute-done
  23.8 0.1 pad_add_fusion.3
  23.9 69.9 %all-gather.2.cloned.1.call-done = bf16[3,2048,1024]{2,1,0:T(8,128)(2,1)} async-done(((bf16[3,128,1024]{2,1,0:T(8,128)(2,1)}), bf16[3,2048,1024]{2,1,0:T(8,128)(2,1)}) %all-gather.2.cloned.1.call-update) | async-done | bytes 12582928 | tf_op jit(solution)/shard_map/all_gather | solution.py:46
  93.8 6.6 convolution_bitcast_fusion.1
  100.5 0.0 copy-start.3
  100.5 0.0 copy-start.4
  100.5 0.0 copy-start.1
  100.5 1.5 copy-done
  102.0 1.9 convolution_bitcast_fusion
  103.9 0.3 fusion.15
  104.2 0.4 fusion.43
  104.6 24.7 %psum.98 = f32[1024]{0:T(1024)S(1)} all-reduce(f32[1024]{0:T(1024)S(1)} %bitcast.94), channel_id=1, replica_groups=mesh['dp'=16,'cell'=32] {'dp'}, use_global_device_ids=true, to_apply=%region_0.1 | all-reduce | flops 1024 | bytes 8192 | tf_op jit(solution)/shard_map/psum | solution.py:104
  129.3 2.4 collective-permute-start.3
  131.7 3.4 collective-permute-start.4
  135.1 0.1 fusion.30
  135.2 0.1 fusion.29
  135.3 0.5 convolution_bitcast_fusion.5
  135.8 71.2 %psum.100 = f32[128]{0:T(128)S(1)} all-reduce(f32[128]{0:T(128)S(1)} %convolution_bitcast_fusion.5), channel_id=1, replica_groups=mesh['dp'=16,'cell'=32] {'cell'}, use_global_device_ids=true, to_apply=%region_3.4 | all-reduce | flops 128 | bytes 1024 | tf_op jit(solution)/shard_map/psum | solution.py:110
  207.0 0.4 fusion.41
  207.4 23.5 %psum.101 = f32[1024]{0:T(1024)S(1)} all-reduce(f32[1024]{0:T(1024)S(1)} %bitcast.91), channel_id=1, replica_groups=mesh['dp'=16,'cell'=32] {'dp'}, use_global_device_ids=true, to_apply=%region_4.5 | all-reduce | flops 1024 | bytes 8192 | tf_op jit(solution)/shard_map/psum | solution.py:104
  231.0 0.1 pad_add_fusion.2
  231.1 0.6 multiply_reduce_fusion.4
  231.7 72.9 %all-reduce.16 = (f32[]{:T(128)}, f32[]{:T(128)}) all-reduce(f32[]{:T(128)} %get-tuple-element.3, f32[]{:T(128)} %get-tuple-element.2), channel_id=1, replica_groups=mesh['dp'=16,'cell'=32] {'cell'}, use_global_device_ids=true, to_apply=%region_2.3 | all-reduce | flops 2 | bytes 16 | tf_op jit(solution)/shard_map/psum | solution.py:107
  305.9 0.6 multiply_reduce_fusion.3
  306.5 70.2 %psum.103 = f32[]{:T(128)} all-reduce(f32[]{:T(128)} %get-tuple-element.8), channel_id=1, replica_groups=mesh['dp'=16,'cell'=32] {'cell'}, use_global_device_ids=true, to_apply=%region_8.9 | all-reduce | flops 1 | bytes 8 | tf_op jit(solution)/shard_map/psum | solution.py:107
  378.1 3.9 collective-permute-start.5
  382.1 1.9 collective-permute-start.6
  384.0 0.1 fusion.25
  384.1 0.1 fusion.26
  384.2 0.5 convolution_bitcast_fusion.4
  384.7 71.6 %psum.104 = f32[128]{0:T(128)S(1)} all-reduce(f32[128]{0:T(128)S(1)} %convolution_bitcast_fusion.4), channel_id=1, replica_groups=mesh['dp'=16,'cell'=32] {'cell'}, use_global_device_ids=true, to_apply=%region_9.10 | all-reduce | flops 128 | bytes 1024 | tf_op jit(solution)/shard_map/psum | solution.py:110
  456.3 0.4 fusion.39
  456.7 23.5 %psum.105 = f32[1024]{0:T(1024)S(1)} all-reduce(f32[1024]{0:T(1024)S(1)} %bitcast.92), channel_id=1, replica_groups=mesh['dp'=16,'cell'=32] {'dp'}, use_global_device_ids=true, to_apply=%region_10.11 | all-reduce | flops 1024 | bytes 8192 | tf_op jit(solution)/shard_map/psum | solution.py:104
  480.3 0.1 pad_add_fusion.1
  480.3 0.6 multiply_reduce_fusion.2
  481.0 70.3 %psum.106 = f32[]{:T(128)} all-reduce(f32[]{:T(128)} %multiply_reduce_fusion.2), channel_id=1, replica_groups=mesh['dp'=16,'cell'=32] {'cell'}, use_global_device_ids=true, to_apply=%region_12.13 | all-reduce | flops 1 | bytes 8 | tf_op jit(solution)/shard_map/psum | solution.py:107
  552.5 0.6 multiply_reduce_fusion.1
  553.1 72.2 %psum.107 = f32[]{:T(128)} all-reduce(f32[]{:T(128)} %get-tuple-element.6), channel_id=1, replica_groups=mesh['dp'=16,'cell'=32] {'cell'}, use_global_device_ids=true, to_apply=%region_14.15 | all-reduce | flops 1 | bytes 8 | tf_op jit(solution)/shard_map/psum | solution.py:107
  626.7 1.9 collective-permute-start.7
  628.7 3.9 collective-permute-start.8
  632.6 0.1 fusion.21
  632.7 0.1 fusion.22
  632.8 0.5 convolution_bitcast_fusion.3
  633.3 69.6 %psum.108 = f32[128]{0:T(128)S(1)} all-reduce(f32[128]{0:T(128)S(1)} %convolution_bitcast_fusion.3), channel_id=1, replica_groups=mesh['dp'=16,'cell'=32] {'cell'}, use_global_device_ids=true, to_apply=%region_15.16 | all-reduce | flops 128 | bytes 1024 | tf_op jit(solution)/shard_map/psum | solution.py:110
  702.9 0.4 fusion.37
  703.3 23.5 %psum.109 = f32[1024]{0:T(1024)S(1)} all-reduce(f32[1024]{0:T(1024)S(1)} %bitcast.93), channel_id=1, replica_groups=mesh['dp'=16,'cell'=32] {'dp'}, use_global_device_ids=true, to_apply=%region_16.17 | all-reduce | flops 1024 | bytes 8192 | tf_op jit(solution)/shard_map/psum | solution.py:104
  726.9 0.1 pad_add_fusion
  726.9 0.6 multiply_reduce_fusion
  727.6 72.3 %psum.110 = f32[]{:T(128)} all-reduce(f32[]{:T(128)} %multiply_reduce_fusion), channel_id=1, replica_groups=mesh['dp'=16,'cell'=32] {'cell'}, use_global_device_ids=true, to_apply=%region_18.19 | all-reduce | flops 1 | bytes 8 | tf_op jit(solution)/shard_map/psum | solution.py:107
  801.2 0.0 copy-start.2
  801.2 0.5 convolution_bitcast_fusion.2
  801.7 70.1 %psum.111 = f32[128]{0:T(128)} all-reduce(f32[128]{0:T(128)S(1)} %convolution_bitcast_fusion.2), channel_id=1, replica_groups=mesh['dp'=16,'cell'=32] {'cell'}, use_global_device_ids=true, to_apply=%region_19.20 | all-reduce | flops 128 | bytes 1024 | tf_op jit(solution)/shard_map/psum | solution.py:110
  (26 shorter events, 0.2 us)
Async XLA Ops:
  7.2 86.7 %all-gather.2.cloned.1.call-start = ((), (), s32[]{:S(2)}) async-start(), calls=%async_computation | async-start | bytes 13369344 | tf_op jit(solution)/shard_map/all_gather | solution.py:46
  7.9 14.8 %collective-permute-start.1 = (f32[1024]{0:T(1024)}, f32[1024]{0:T(1024)S(1)}, u32[]{:S(2)}, u32[]{:S(2)}) collective-permute-start(f32[1024]{0:T(1024)} %param.10), channel_id=1, source_target_pairs={{1,0},{2,1},{3,2},{4,3},{5,4},{6,5},{7,6},{8,7},{9,8},{10,9},{11,1... | collective-permute-start | bytes 12296 | tf_op jit(solution)/shard_map/ppermute | solution.py:32
  15.6 7.1 collective-permute-start.2
  18.3 5.5 collective-permute-start
  93.8 8.2 copy-start
  100.5 3.7 copy-start.3
  100.5 3.7 copy-start.4
  100.5 34.6 %copy-start.1 = (f32[3,1024]{1,0:T(4,128)S(1)}, f32[3,1024]{1,0:T(4,128)}, u32[]{:S(2)}) copy-start(f32[3,1024]{1,0:T(4,128)} %param.11) | copy-start | bytes 36868
  129.3 101.7 %collective-permute-start.3 = (f32[1024]{0:T(1024)S(1)}, f32[1024]{0:T(1024)S(1)}, u32[]{:S(2)}, u32[]{:S(2)}) collective-permute-start(f32[1024]{0:T(1024)S(1)} %sub.108), channel_id=1, source_target_pairs={{1,0},{2,1},{3,2},{4,3},{5,4},{6,5},{7,6},{8,7},{9,8},{10,9},{11,1... | collective-permute-start | bytes 12296 | tf_op jit(solution)/shard_map/ppermute | solution.py:32
  131.7 99.2 %collective-permute-start.4 = (f32[1024]{0:T(1024)S(1)}, f32[1024]{0:T(1024)S(1)}, u32[]{:S(2)}, u32[]{:S(2)}) collective-permute-start(f32[1024]{0:T(1024)S(1)} %sub.108), channel_id=1, source_target_pairs={{0,1},{1,2},{2,3},{3,4},{4,5},{5,6},{6,7},{7,8},{8,9},{9,10},{10,1... | collective-permute-start | bytes 12296 | tf_op jit(solution)/shard_map/ppermute | solution.py:30
  378.1 102.1 %collective-permute-start.5 = (f32[1024]{0:T(1024)S(1)}, f32[1024]{0:T(1024)S(1)}, u32[]{:S(2)}, u32[]{:S(2)}) collective-permute-start(f32[1024]{0:T(1024)S(1)} %multiply_add_fusion.2), channel_id=1, source_target_pairs={{1,0},{2,1},{3,2},{4,3},{5,4},{6,5},{7,6},{8,7},{9,8},{10,9},{11,1... | collective-permute-start | bytes 12296 | tf_op jit(solution)/shard_map/ppermute | solution.py:32
  382.1 98.1 %collective-permute-start.6 = (f32[1024]{0:T(1024)S(1)}, f32[1024]{0:T(1024)S(1)}, u32[]{:S(2)}, u32[]{:S(2)}) collective-permute-start(f32[1024]{0:T(1024)S(1)} %multiply_add_fusion.2), channel_id=1, source_target_pairs={{0,1},{1,2},{2,3},{3,4},{4,5},{5,6},{6,7},{7,8},{8,9},{9,10},{10,1... | collective-permute-start | bytes 12296 | tf_op jit(solution)/shard_map/ppermute | solution.py:30
  626.7 100.1 %collective-permute-start.7 = (f32[1024]{0:T(1024)S(1)}, f32[1024]{0:T(1024)S(1)}, u32[]{:S(2)}, u32[]{:S(2)}) collective-permute-start(f32[1024]{0:T(1024)S(1)} %multiply_add_fusion.1), channel_id=1, source_target_pairs={{1,0},{2,1},{3,2},{4,3},{5,4},{6,5},{7,6},{8,7},{9,8},{10,9},{11,1... | collective-permute-start | bytes 12296 | tf_op jit(solution)/shard_map/ppermute | solution.py:32
  628.7 98.1 %collective-permute-start.8 = (f32[1024]{0:T(1024)S(1)}, f32[1024]{0:T(1024)S(1)}, u32[]{:S(2)}, u32[]{:S(2)}) collective-permute-start(f32[1024]{0:T(1024)S(1)} %multiply_add_fusion.1), channel_id=1, source_target_pairs={{0,1},{1,2},{2,3},{3,4},{4,5},{5,6},{6,7},{7,8},{8,9},{9,10},{10,1... | collective-permute-start | bytes 12296 | tf_op jit(solution)/shard_map/ppermute | solution.py:30
  801.2 70.7 %copy-start.2 = (f32[1024]{0:T(1024)}, f32[1024]{0:T(1024)S(1)}, u32[]{:S(2)}) copy-start(f32[1024]{0:T(1024)S(1)} %multiply_add_fusion) | copy-start | bytes 12292
Sparse Core Ops, SparseCore 0:
  10.1 83.6 all-gather.1
where the time goes:
time: 880 us; the launch traced here: 879 us
  blocking collectives  736 us (84%)
  waiting for transfers between devices  70.9 us (8%)
  starting transfers between devices  29.1 us (3%)
  between operations  21 us (2%)
  matrix products  12.1 us (1%)
    psum x5, blocking collectives, global_sum(): return lax.psum(values, 'cell')  358 us
    psum x4, blocking collectives, data_image(): return lax.psum(jnp.dot(sensitivity, whole, precision=high), 'cell')  283 us
    psum x4, blocking collectives, spread(): return lax.psum(model_term, 'dp')  95.3 us
    all_gather x1, waiting for transfers between devices, per_device(): fields_part = lax.all_gather(pole_fields, 'dp', axis=1, tiled=True)  69.9 us
  transfers between devices with their start and end apart: 10, of which 2 were waited for; matrix products, arithmetic and copies ran while one was open for 1% of the time, Pallas kernels for 0%

commit v1 on v0

v1 whole, which is shorter than its diff:
```python
import functools
import math

import jax
import jax.numpy as jnp
from jax import lax
from jax.experimental import pallas as pl
from jax.experimental.pallas import tpu as pltpu
from jax.sharding import PartitionSpec as P

GY = 32
GZ = 32
ITERS = 3
DAMPING = 0.2

DP = 16
CELL = 32
OWN = 64
POLE_ROWS = 128
CHUNK = 256
DATA = 2048
LANES = 128
F32 = jnp.float32
BF16 = jnp.bfloat16
MESH = pl.DeviceIdType.MESH


def lane_sum(row):
    return jnp.sum(row, axis=1, keepdims=True)


def kernel(
    fields,
    configs_t,
    misfit,
    weight,
    conductivity,
    faces,
    update_out,
    change_out,
    field_out,
    field_in,
    signs,
    totals,
    sens,
    setup_out,
    setup_in,
    static_out,
    static_in,
    first_out,
    first_in,
    plane_out,
    plane_in,
    second_out,
    second_in,
    third_in,
    field_send,
    field_recv,
    send_sems,
    recv_sems,
):
    dp = lax.axis_index("dp")
    cell = lax.axis_index("cell")
    chip = dp // 2
    core = dp % 2
    above = (cell + 1) % CELL
    below = (cell + CELL - 1) % CELL

    barrier = pltpu.get_barrier_semaphore()
    for step in range(1, DP):
        pl.semaphore_signal(
            barrier, inc=1, device_id={"dp": (dp + step) % DP, "cell": cell}, device_id_type=MESH
        )
    for step in range(1, CELL):
        pl.semaphore_signal(
            barrier, inc=1, device_id={"dp": dp, "cell": (cell + step) % CELL}, device_id_type=MESH
        )

    lane = lax.broadcasted_iota(jnp.int32, (1, LANES), 1)
    own = (lane >= 32) & (lane < 96)

    for target in range(8):
        for part in range(3):
            turned = fields[part, :, target * LANES : (target + 1) * LANES].T
            field_out[2 * target, part * OWN : (part + 1) * OWN, :] = turned[:OWN]
            field_out[2 * target + 1, part * OWN : (part + 1) * OWN, :] = turned[OWN:]
    field_in[dp] = field_out[dp]

    setup_out[0:4, :] = configs_t[...].astype(F32)
    setup_out[4:5, :] = weight[...]
    setup_out[5:6, :] = misfit[...]
    setup_out[6:8, :] = jnp.zeros((2, LANES), F32)
    setup_in[dp] = setup_out[...]

    even = dp % 2 == 0
    tile_a = jnp.maximum((dp + 1) // 2 - 1, 0)
    tile_b = jnp.minimum((dp + 1) // 2, 7)

    def widened(first, second):
        if_even = jnp.where(lane < 32, pltpu.roll(first, 32, 1), pltpu.roll(second, 32, 1))
        if_odd = jnp.where(lane < 96, pltpu.roll(first, 96, 1), pltpu.roll(second, 96, 1))
        return jnp.where(jnp.broadcast_to(even, (1, LANES)), if_even, if_odd)

    def face_row(axis):
        return widened(
            faces[axis : axis + 1, pl.ds(pl.multiple_of(tile_a * LANES, LANES), LANES)],
            faces[axis : axis + 1, pl.ds(pl.multiple_of(tile_b * LANES, LANES), LANES)],
        )

    cond_row = widened(conductivity[pl.ds(tile_a, 1), :], conductivity[pl.ds(tile_b, 1), :])
    face_x, face_y, face_z = face_row(0), face_row(1), face_row(2)
    static_out[0:1, :] = cond_row
    static_out[1:2, :] = face_x

    totals[...] = jnp.zeros(totals.shape, F32)

    pl.semaphore_wait(barrier, DP - 1 + CELL - 1)

    def push(source, target, send, recv, to_dp, to_cell):
        pltpu.make_async_remote_copy(
            src_ref=source,
            dst_ref=target,
            send_sem=send,
            recv_sem=recv,
            device_id={"dp": to_dp, "cell": to_cell},
            device_id_type=MESH,
        ).start()

    def await_bytes(ref, sem):
        pltpu.make_async_copy(ref, ref, sem).wait()

    for step in range(1, DP):
        push(setup_out, setup_in.at[dp], send_sems.at[0], recv_sems.at[0], (dp + step) % DP, cell)
    push(static_out, static_in.at[0], send_sems.at[1], recv_sems.at[1], dp, above)
    push(static_out, static_in.at[1], send_sems.at[1], recv_sems.at[1], dp, below)
    for far in (4, 3, 5, 2, 6, 1, 7, 0):
        for other in (0, 1):
            if (far, other) == (0, 0):
                continue
            to = (chip + far) % 8 * 2 + (core + other) % 2
            push(field_out.at[to], field_in.at[dp], field_send, field_recv.at[dp], to, cell)

    await_bytes(setup_in.at[pl.ds(0, DP - 1)], recv_sems.at[0])

    def one_chunk(step, carry):
        half = (step + 1) // 2
        chunk = (chip + (8 - half) % 8 + (step % 2) * (2 * half - 8)) % 8
        ids = (lax.broadcasted_iota(jnp.int32, (CHUNK, 1), 0) + chunk * CHUNK).astype(F32)

        def signs_of(block, inner):
            rows = setup_in[block]
            at = pl.multiple_of(block * LANES, LANES)
            for pair in range(2):
                plus, minus = rows[2 * pair : 2 * pair + 1], rows[2 * pair + 1 : 2 * pair + 2]
                value = jnp.where(ids == plus, 1.0, jnp.where(ids == minus, -1.0, 0.0))
                signs[:, pl.ds(pl.multiple_of(pair * DATA + at, LANES), LANES)] = value.astype(BF16)
            return inner

        lax.fori_loop(0, DP, signs_of, 0)

        def wait_field(source):
            @pl.when(source != dp)
            def _():
                await_bytes(field_in.at[source], field_recv.at[source])

        wait_field(2 * chunk)
        wait_field(2 * chunk + 1)
        left = jnp.concatenate([field_in[2 * chunk], field_in[2 * chunk + 1]], axis=1)

        def product(tile, inner):
            at = pl.ds(pl.multiple_of(tile * 512, 512), 512)
            totals[:, at] += jnp.dot(left, signs[:, at], preferred_element_type=F32)
            return inner

        lax.fori_loop(0, 8, product, 0)
        return carry

    lax.fori_loop(0, 8, one_chunk, 0)

    scale = -1.0 / math.sqrt(DATA)
    gradient_sum = jnp.zeros((OWN, LANES), F32)
    for block in range(DP):
        at, bt = block * LANES, DATA + block * LANES
        value = totals[0:OWN, at : at + LANES] * totals[0:OWN, bt : bt + LANES]
        for part in (1, 2):
            rows = slice(part * OWN, (part + 1) * OWN)
            value += totals[rows, at : at + LANES] * totals[rows, bt : bt + LANES]
        value = value * scale
        sens[block] = value
        gradient_sum += value * (setup_in[block, 4:5, :] * setup_in[block, 5:6, :])

    spot = lax.broadcasted_iota(jnp.int32, (OWN, LANES), 0) + 32 == lax.broadcasted_iota(
        jnp.int32, (OWN, LANES), 1
    )

    def to_row(spread):
        column = jnp.sum(spread, axis=1, keepdims=True)
        return jnp.sum(jnp.where(spot, column, 0.0), axis=0, keepdims=True)

    def to_column(row):
        return jnp.sum(jnp.where(spot, row, 0.0), axis=1, keepdims=True)

    await_bytes(static_in, recv_sems.at[1])

    def masked(row, keep):
        return jnp.where(own & keep, row, 0.0)

    grid_y = 2 * dp + (lane - 32) // 32
    grid_z = lane % 32
    up_x = masked(face_x, jnp.broadcast_to(cell < CELL - 1, (1, LANES)))
    low_x = masked(static_in[0, 1:2, :], jnp.broadcast_to(cell > 0, (1, LANES)))
    up_y = masked(face_y, grid_y < GY - 1)
    low_y = masked(pltpu.roll(face_y, 32, 1), grid_y > 0)
    up_z = masked(face_z, grid_z < GZ - 1)
    low_z = masked(pltpu.roll(face_z, 1, 1), grid_z > 0)

    def roughness(row, lower, upper):
        return (
            up_x * (row - upper)
            + low_x * (row - lower)
            + up_y * (row - pltpu.roll(row, 96, 1))
            + low_y * (row - pltpu.roll(row, 32, 1))
            + up_z * (row - pltpu.roll(row, 127, 1))
            + low_z * (row - pltpu.roll(row, 1, 1))
        )

    residual = to_row(gradient_sum) - roughness(cond_row, static_in[0, 0:1, :], static_in[1, 0:1, :])
    residual = jnp.where(own, residual, 0.0)

    for it in range(ITERS):
        sem = 2 + 4 * it
        column = jnp.broadcast_to(to_column(residual), (OWN, LANES))
        plane_out[it] = residual
        push(plane_out.at[it], plane_in.at[it, 0], send_sems.at[sem], recv_sems.at[sem], dp, above)
        push(plane_out.at[it], plane_in.at[it, 1], send_sems.at[sem], recv_sems.at[sem], dp, below)
        for block in range(DP):
            image_row = jnp.sum(sens[block] * column, axis=0, keepdims=True)
            first_out[it, block] = jnp.concatenate([image_row, residual], axis=0)
        for step in (8, 7, 9, 6, 10, 5, 11, 4, 12, 3, 13, 2, 14, 1, 15):
            to = (dp + step) % DP
            push(
                first_out.at[it, to],
                first_in.at[it, dp],
                send_sems.at[sem + 1],
                recv_sems.at[sem + 1],
                to,
                cell,
            )
        first_in[it, dp] = first_out[it, dp]
        await_bytes(plane_in.at[it], recv_sems.at[sem])
        await_bytes(first_in.at[it, pl.ds(0, DP - 1)], recv_sems.at[sem + 1])
        gathered = first_in[it]
        partial = jnp.sum(gathered[:, 0:1, :], axis=0)
        before = first_in[it, (dp + DP - 1) % DP][1:2, :]
        after = first_in[it, (dp + 1) % DP][1:2, :]
        wide = jnp.where(
            own, residual, pltpu.roll(jnp.where(lane >= 64, before, after), 64, 1)
        )
        rough = roughness(wide, plane_in[it, 0], plane_in[it, 1]) + DAMPING * residual
        scalars = jnp.where(lane == 0, lane_sum(residual * residual), 0.0)
        scalars = jnp.where(lane == 1, lane_sum(residual * rough), scalars)
        if it > 0:
            scalars = jnp.where(lane == 2, lane_sum(residual * direction_rough), scalars)
        message = jnp.concatenate([partial, scalars], axis=0)
        second_out[it] = message
        for step in range(1, CELL):
            push(
                second_out.at[it],
                second_in.at[it, step - 1],
                send_sems.at[sem + 2],
                recv_sems.at[sem + 2],
                dp,
                (cell + step) % CELL,
            )
        await_bytes(second_in.at[it], recv_sems.at[sem + 2])
        message = message + jnp.sum(second_in[it], axis=0)
        third_in[it, dp] = message
        for step in (8, 7, 9, 6, 10, 5, 11, 4, 12, 3, 13, 2, 14, 1, 15):
            push(
                third_in.at[it, dp],
                third_in.at[it, dp],
                send_sems.at[sem + 3],
                recv_sems.at[sem + 3],
                (dp + step) % DP,
                cell,
            )
        await_bytes(third_in.at[it, pl.ds(0, DP - 1)], recv_sems.at[sem + 3])
        sums = jnp.sum(third_in[it][:, 1:2, :], axis=0)
        norm_next = sums[:, 0:1]
        energy = sums[:, 1:2]
        plane_rows = gathered[:, 1, :]
        if it == 0:
            predicted = [third_in[it, block][0:1, :] for block in range(DP)]
            direction_rough = rough
            predicted_own = message[0:1, :]
            whole = plane_rows
        else:
            ratio = norm_next / norm_now
            energy = energy + ratio * (2.0 * sums[:, 2:3] + ratio * energy_before)
            predicted = [
                third_in[it, block][0:1, :] + ratio * predicted[block] for block in range(DP)
            ]
            direction_rough = rough + ratio * direction_rough
            predicted_own = message[0:1, :] + ratio * predicted_own
            whole = plane_rows + ratio * whole
        weighted = [setup_in[block, 4:5, :] * predicted[block] for block in range(DP)]
        square = weighted[0] * predicted[0]
        for block in range(1, DP):
            square += weighted[block] * predicted[block]
        step_length = norm_next / (energy + lane_sum(square))
        if it == 0:
            update = step_length * whole
            change = step_length * predicted_own
        else:
            update = update + step_length * whole
            change = change + step_length * predicted_own
        if it < ITERS - 1:
            spread = sens[0] * weighted[0]
            for block in range(1, DP):
                spread += sens[block] * weighted[block]
            image = to_row(spread) + direction_rough
            residual = jnp.where(own, residual - step_length * image, 0.0)
        norm_now = norm_next
        energy_before = energy

    update_out[...] = update
    change_out[...] = change

    await_bytes(setup_in.at[pl.ds(0, DP - 1)], send_sems.at[0])
    await_bytes(static_in, send_sems.at[1])
    await_bytes(field_in.at[pl.ds(0, DP - 1)], field_send)
    for it in range(ITERS):
        sem = 2 + 4 * it
        await_bytes(plane_in.at[it], send_sems.at[sem])
        await_bytes(first_in.at[it, pl.ds(0, DP - 1)], send_sems.at[sem + 1])
        await_bytes(second_in.at[it], send_sems.at[sem + 2])
        await_bytes(third_in.at[it, pl.ds(0, DP - 1)], send_sems.at[sem + 3])


def per_device(configs, pole_fields, misfit, data_weight, conductivity, face_weights):
    vmem = pl.BlockSpec(memory_space=pltpu.VMEM)
    update, change = pl.pallas_call(
        kernel,
        name="inversion",
        out_shape=(
            jax.ShapeDtypeStruct((DP, LANES), F32),
            jax.ShapeDtypeStruct((1, LANES), F32),
        ),
        in_specs=[vmem] * 6,
        out_specs=(vmem, vmem),
        scratch_shapes=[
            pltpu.VMEM((DP, 3 * OWN, POLE_ROWS), BF16),
            pltpu.VMEM((DP, 3 * OWN, POLE_ROWS), BF16),
            pltpu.VMEM((CHUNK, 2 * DATA), BF16),
            pltpu.VMEM((3 * OWN, 2 * DATA), F32),
            pltpu.VMEM((DP, OWN, LANES), F32),
            pltpu.VMEM((8, LANES), F32),
            pltpu.VMEM((DP, 8, LANES), F32),
            pltpu.VMEM((2, LANES), F32),
            pltpu.VMEM((2, 2, LANES), F32),
            pltpu.VMEM((ITERS, DP, 2, LANES), F32),
            pltpu.VMEM((ITERS, DP, 2, LANES), F32),
            pltpu.VMEM((ITERS, 1, LANES), F32),
            pltpu.VMEM((ITERS, 2, 1, LANES), F32),
            pltpu.VMEM((ITERS, 2, LANES), F32),
            pltpu.VMEM((ITERS, CELL - 1, 2, LANES), F32),
            pltpu.VMEM((ITERS, DP, 2, LANES), F32),
            pltpu.SemaphoreType.DMA,
            pltpu.SemaphoreType.DMA((DP,)),
            pltpu.SemaphoreType.DMA((2 + 4 * ITERS,)),
            pltpu.SemaphoreType.DMA((2 + 4 * ITERS,)),
        ],
        compiler_params=pltpu.CompilerParams(
            collective_id=0, has_side_effects=True, vmem_limit_bytes=40 * 1024 * 1024
        ),
    )(
        pole_fields,
        configs.T,
        misfit.reshape(1, LANES),
        data_weight.reshape(1, LANES),
        conductivity.reshape(8, LANES),
        face_weights,
    )
    return update[:, 32:96].reshape(-1), change.reshape(-1)


def solution(mesh):
    placed = (P("dp", None), P(None, "dp", "cell"), P("dp"), P("dp"), P("cell"), P(None, "cell"))
    return jax.shard_map(
        per_device, mesh=mesh, in_specs=placed, out_specs=(P("cell"), P("dp")), check_vma=False
    )
```

time: 880 us -> 105 us (0.12)
  the two profiles are of different devices: /device:TPU:8 before, /device:TPU:1 now
where the time goes in v1:
time: 105 us
  Pallas kernels  100 us (95%)
  local copies, waits for them, and re-layouts  3.77 us (4%)
    pallas_call x1, Pallas kernels, per_device(): pl.pallas_call(kernel, name='inversion', out_shape=(jax.ShapeDtypeStruct(...  100 us
    unnamed x13, local copies, waits for them, and re-layouts  3.03 us

profile of v1, /device:TPU:1, one launch (start us, length us, event | category | flops | bytes accessed | tf_op | source)
XLA Modules:
  0.0 104.6 jit_solution(1993278789418879056)
XLA Ops:
  0.6 0.0 copy-start.2
  0.6 0.0 copy-start.3
  0.7 0.0 copy-start.4
  0.7 0.0 copy-start.5
  0.7 0.6 copy-done.2
  1.3 0.0 copy-done.3
  1.3 0.0 copy-done.4
  1.3 0.0 copy-done.5
  1.3 0.0 copy-start
  1.3 1.1 %copy-done = bf16[3,128,1024]{2,1,0:T(8,128)(2,1)S(1)} copy-done((bf16[3,128,1024]{2,1,0:T(8,128)(2,1)S(1)}, bf16[3,128,1024]{2,1,0:T(8,128)(2,1)}, u32[]{:S(2)}) %copy-start) | copy-done | bytes 786456
  2.5 0.0 copy-start.1
  2.5 0.7 copy-done.1
  3.2 100.1 %inversion.1 = (f32[16,128]{1,0:T(8,128)S(1)}, f32[1,128]{1,0:T(1,128)S(1)}) custom-call(bf16[3,128,1024]{2,1,0:T(8,128)(2,1)S(1)} %copy-done, s32[4,128]{1,0:T(4,128)S(1)} %bitcast.6, f32[1,128]{1,0:T(1,128)S(1)} %bitcast.7, f32[1,128]{1,0:T(1,128)S(1)} %bitcast.8, f32[8,128]{1,0:T(8,128)S(1)} %bitcast.5, f32[3,1024]{1,0:T(4,128)S(1)} %copy-done.1), custom_call_target="tpu_custom_call" | custom-call | tf_op jit(solution)/shard_map/inversion/pallas_call | solution.py:342
  103.3 0.1 slice.3
  103.4 0.7 reshape.22
  104.1 0.5 copy.9
Async XLA Ops:
  0.6 0.7 copy-start.2
  0.6 0.7 copy-start.3
  0.7 0.7 copy-start.4
  0.7 0.7 copy-start.5
  1.3 1.1 %copy-start = (bf16[3,128,1024]{2,1,0:T(8,128)(2,1)S(1)}, bf16[3,128,1024]{2,1,0:T(8,128)(2,1)}, u32[]{:S(2)}) copy-start(bf16[3,128,1024]{2,1,0:T(8,128)(2,1)} %fields.1) | copy-start | bytes 2359300
  2.5 0.7 copy-start.1

commit v2 on v1

--- a/solution.py
+++ b/solution.py
@@ -30,17 +30,24 @@
 
 
 def kernel(
+    fields_hbm,
+    configs_hbm,
+    misfit_hbm,
+    weight_hbm,
+    conductivity_hbm,
+    faces_hbm,
+    update_out,
+    change_out,
     fields,
     configs_t,
     misfit,
     weight,
     conductivity,
     faces,
-    update_out,
-    change_out,
     field_out,
     field_in,
-    signs,
+    signs_a,
+    signs_b,
     totals,
     sens,
     setup_out,
@@ -58,7 +65,22 @@
     field_recv,
     send_sems,
     recv_sems,
+    load_sems,
 ):
+    loads = []
+    for index, (source, target) in enumerate(
+        (
+            (fields_hbm, fields),
+            (configs_hbm, configs_t),
+            (weight_hbm, weight),
+            (misfit_hbm, misfit),
+            (conductivity_hbm, conductivity),
+            (faces_hbm, faces),
+        )
+    ):
+        loads.append(pltpu.make_async_copy(source, target, load_sems.at[index]))
+        loads[-1].start()
+
     dp = lax.axis_index("dp")
     cell = lax.axis_index("cell")
     chip = dp // 2
@@ -79,6 +101,9 @@
     lane = lax.broadcasted_iota(jnp.int32, (1, LANES), 1)
     own = (lane >= 32) & (lane < 96)
 
+    for load in loads:
+        load.wait()
+
     for target in range(8):
         for part in range(3):
             turned = fields[part, :, target * LANES : (target + 1) * LANES].T
@@ -111,8 +136,6 @@
     face_x, face_y, face_z = face_row(0), face_row(1), face_row(2)
     static_out[0:1, :] = cond_row
     static_out[1:2, :] = face_x
-
-    totals[...] = jnp.zeros(totals.shape, F32)
 
     pl.semaphore_wait(barrier, DP - 1 + CELL - 1)
 
@@ -133,7 +156,7 @@
         push(setup_out, setup_in.at[dp], send_sems.at[0], recv_sems.at[0], (dp + step) % DP, cell)
     push(static_out, static_in.at[0], send_sems.at[1], recv_sems.at[1], dp, above)
     push(static_out, static_in.at[1], send_sems.at[1], recv_sems.at[1], dp, below)
-    for far in (4, 3, 5, 2, 6, 1, 7, 0):
+    for far in (1, 7, 2, 6, 3, 5, 4, 0):
         for other in (0, 1):
             if (far, other) == (0, 0):
                 continue
@@ -142,40 +165,50 @@
 
     await_bytes(setup_in.at[pl.ds(0, DP - 1)], recv_sems.at[0])
 
-    def one_chunk(step, carry):
+    def chunk_of(step):
         half = (step + 1) // 2
-        chunk = (chip + (8 - half) % 8 + (step % 2) * (2 * half - 8)) % 8
-        ids = (lax.broadcasted_iota(jnp.int32, (CHUNK, 1), 0) + chunk * CHUNK).astype(F32)
-
-        def signs_of(block, inner):
-            rows = setup_in[block]
-            at = pl.multiple_of(block * LANES, LANES)
+        return (chip + (8 - half) % 8 + (step % 2) * (2 * half - 8)) % 8
+
+    def build(signs, step):
+        ids = lax.broadcasted_iota(jnp.int32, (CHUNK, 1), 0) + chunk_of(step) * CHUNK
+        ids = jnp.broadcast_to(ids.astype(F32), (CHUNK, LANES))
+        for block in range(DP):
             for pair in range(2):
-                plus, minus = rows[2 * pair : 2 * pair + 1], rows[2 * pair + 1 : 2 * pair + 2]
+                plus = setup_in[block, 2 * pair : 2 * pair + 1, :]
+                minus = setup_in[block, 2 * pair + 1 : 2 * pair + 2, :]
                 value = jnp.where(ids == plus, 1.0, jnp.where(ids == minus, -1.0, 0.0))
-                signs[:, pl.ds(pl.multiple_of(pair * DATA + at, LANES), LANES)] = value.astype(BF16)
-            return inner
-
-        lax.fori_loop(0, DP, signs_of, 0)
-
-        def wait_field(source):
-            @pl.when(source != dp)
-            def _():
-                await_bytes(field_in.at[source], field_recv.at[source])
-
-        wait_field(2 * chunk)
-        wait_field(2 * chunk + 1)
+                at = pair * DATA + block * LANES
+                signs[:, at : at + LANES] = value.astype(BF16)
+
+    def product(signs, step):
+        chunk = chunk_of(step)
         left = jnp.concatenate([field_in[2 * chunk], field_in[2 * chunk + 1]], axis=1)
-
-        def product(tile, inner):
-            at = pl.ds(pl.multiple_of(tile * 512, 512), 512)
-            totals[:, at] += jnp.dot(left, signs[:, at], preferred_element_type=F32)
-            return inner
-
-        lax.fori_loop(0, 8, product, 0)
+        return jnp.dot(left, signs[...], preferred_element_type=F32)
+
+    def await_fields(step):
+        for part in range(2):
+            source = 2 * chunk_of(step) + part
+            await_bytes(field_in.at[source], field_recv.at[source])
+
+    build(signs_a, 0)
+    sibling = 2 * chip + 1 - core
+    await_bytes(field_in.at[sibling], field_recv.at[sibling])
+    totals[...] = product(signs_a, 0)
+    build(signs_b, 1)
+
+    def two_chunks(turn, carry):
+        for signs, later, step in (
+            (signs_b, signs_a, 2 * turn + 1),
+            (signs_a, signs_b, 2 * turn + 2),
+        ):
+            await_fields(step)
+            totals[...] += product(signs, step)
+            build(later, step + 1)
         return carry
 
-    lax.fori_loop(0, 8, one_chunk, 0)
+    lax.fori_loop(0, 3, two_chunks, 0)
+    await_fields(7)
+    totals[...] += product(signs_b, 7)
 
     scale = -1.0 / math.sqrt(DATA)
     gradient_sum = jnp.zeros((OWN, LANES), F32)
@@ -346,11 +379,18 @@
             jax.ShapeDtypeStruct((DP, LANES), F32),
             jax.ShapeDtypeStruct((1, LANES), F32),
         ),
-        in_specs=[vmem] * 6,
+        in_specs=[pl.BlockSpec(memory_space=pltpu.HBM)] * 6,
         out_specs=(vmem, vmem),
         scratch_shapes=[
+            pltpu.VMEM((3, POLE_ROWS, 8 * LANES), BF16),
+            pltpu.VMEM((4, LANES), jnp.int32),
+            pltpu.VMEM((1, LANES), F32),
+            pltpu.VMEM((1, LANES), F32),
+            pltpu.VMEM((8, LANES), F32),
+            pltpu.VMEM((3, 8 * LANES), F32),
             pltpu.VMEM((DP, 3 * OWN, POLE_ROWS), BF16),
             pltpu.VMEM((DP, 3 * OWN, POLE_ROWS), BF16),
+            pltpu.VMEM((CHUNK, 2 * DATA), BF16),
             pltpu.VMEM((CHUNK, 2 * DATA), BF16),
             pltpu.VMEM((3 * OWN, 2 * DATA), F32),
             pltpu.VMEM((DP, OWN, LANES), F32),
@@ -369,6 +409,7 @@
             pltpu.SemaphoreType.DMA((DP,)),
             pltpu.SemaphoreType.DMA((2 + 4 * ITERS,)),
             pltpu.SemaphoreType.DMA((2 + 4 * ITERS,)),
+            pltpu.SemaphoreType.DMA((6,)),
         ],
         compiler_params=pltpu.CompilerParams(
             collective_id=0, has_side_effects=True, vmem_limit_bytes=40 * 1024 * 1024

time: 105 us -> 91.8 us (0.87)
  Pallas kernels: 100 us -> 87.1 us
    pallas_call x1, Pallas kernels: 100 us -> 87.1 us  [per_device(): pl.pallas_call(kernel, name='inversion', out_shape=(jax.ShapeDtypeStruct(...]
where the time goes in v2:
time: 91.8 us; the launch traced here: 91.6 us
  Pallas kernels  87.1 us (95%)
  local copies, waits for them, and re-layouts  3.77 us (4%)
    pallas_call x1, Pallas kernels, per_device(): pl.pallas_call(kernel, name='inversion', out_shape=(jax.ShapeDtypeStruct(...  87.1 us
    unnamed x13, local copies, waits for them, and re-layouts  3.03 us

profile of v2, /device:TPU:1, one launch (start us, length us, event | category | flops | bytes accessed | tf_op | source)
XLA Modules:
  0.0 91.6 jit_solution(4579254954901947429)
XLA Ops:
  0.6 0.0 copy-start.2
  0.6 0.0 copy-start.3
  0.7 0.0 copy-start.4
  0.7 0.0 copy-start.5
  0.7 0.6 copy-done.2
  1.3 0.0 copy-done.3
  1.3 0.0 copy-done.4
  1.3 0.0 copy-done.5
  1.3 0.0 copy-start
  1.3 1.1 %copy-done = bf16[3,128,1024]{2,1,0:T(8,128)(2,1)S(1)} copy-done((bf16[3,128,1024]{2,1,0:T(8,128)(2,1)S(1)}, bf16[3,128,1024]{2,1,0:T(8,128)(2,1)}, u32[]{:S(2)}) %copy-start) | copy-done | bytes 786456
  2.5 0.0 copy-start.1
  2.5 0.7 copy-done.1
  3.2 87.1 %inversion.1 = (f32[16,128]{1,0:T(8,128)S(1)}, f32[1,128]{1,0:T(1,128)S(1)}) custom-call(bf16[3,128,1024]{2,1,0:T(8,128)(2,1)S(1)} %copy-done, s32[4,128]{1,0:T(4,128)S(1)} %bitcast.6, f32[1,128]{1,0:T(1,128)S(1)} %bitcast.7, f32[1,128]{1,0:T(1,128)S(1)} %bitcast.8, f32[8,128]{1,0:T(8,128)S(1)} %bitcast.5, f32[3,1024]{1,0:T(4,128)S(1)} %copy-done.1), custom_call_target="tpu_custom_call" | custom-call | tf_op jit(solution)/shard_map/inversion/pallas_call | solution.py:375
  90.3 0.1 slice.3
  90.4 0.7 reshape.22
  91.1 0.5 copy.9
Async XLA Ops:
  0.6 0.7 copy-start.2
  0.6 0.7 copy-start.3
  0.7 0.7 copy-start.4
  0.7 0.7 copy-start.5
  1.3 1.1 %copy-start = (bf16[3,128,1024]{2,1,0:T(8,128)(2,1)S(1)}, bf16[3,128,1024]{2,1,0:T(8,128)(2,1)}, u32[]{:S(2)}) copy-start(bf16[3,128,1024]{2,1,0:T(8,128)(2,1)} %fields_hbm.1) | copy-start | bytes 2359300
  2.5 0.7 copy-start.1

commit v3 on v2

--- a/solution.py
+++ b/solution.py
@@ -23,6 +23,10 @@
 F32 = jnp.float32
 BF16 = jnp.bfloat16
 MESH = pl.DeviceIdType.MESH
+
+FAR = (4, 3, 5, 2, 6, 1, 7, 0)
+PLANE = [(c, x, y) for x in (2, 1, 3, 0) for y in FAR for c in (0, 1) if (c, x, y) != (0, 0, 0)]
+COLUMN = [(z, c, y) for z in FAR for y in (1, 0) for c in (0, 1) if (z, c, y) != (0, 0, 0)]
 
 
 def lane_sum(row):
@@ -54,13 +58,13 @@
     setup_in,
     static_out,
     static_in,
+    halo_out,
+    halo_in,
     first_out,
     first_in,
-    plane_out,
-    plane_in,
-    second_out,
     second_in,
-    third_in,
+    scalar_out,
+    scalar_in,
     field_send,
     field_recv,
     send_sems,
@@ -89,14 +93,27 @@
     below = (cell + CELL - 1) % CELL
 
     barrier = pltpu.get_barrier_semaphore()
-    for step in range(1, DP):
+    for to_core, to_x, to_y in PLANE:
         pl.semaphore_signal(
-            barrier, inc=1, device_id={"dp": (dp + step) % DP, "cell": cell}, device_id_type=MESH
+            barrier,
+            inc=1,
+            device_id={
+                "dp": 2 * chip + (core + to_core) % 2,
+                "cell": (cell // 8 + to_x) % 4 * 8 + (cell + to_y) % 8,
+            },
+            device_id_type=MESH,
         )
-    for step in range(1, CELL):
-        pl.semaphore_signal(
-            barrier, inc=1, device_id={"dp": dp, "cell": (cell + step) % CELL}, device_id_type=MESH
-        )
+    for to_z, to_core, to_pair in COLUMN:
+        if to_z != 0:
+            pl.semaphore_signal(
+                barrier,
+                inc=1,
+                device_id={
+                    "dp": (chip + to_z) % 8 * 2 + (core + to_core) % 2,
+                    "cell": cell + to_pair * (1 - 2 * (cell % 2)),
+                },
+                device_id_type=MESH,
+            )
 
     lane = lax.broadcasted_iota(jnp.int32, (1, LANES), 1)
     own = (lane >= 32) & (lane < 96)
@@ -137,7 +154,7 @@
     static_out[0:1, :] = cond_row
     static_out[1:2, :] = face_x
 
-    pl.semaphore_wait(barrier, DP - 1 + CELL - 1)
+    pl.semaphore_wait(barrier, 63 + 28)
 
     def push(source, target, send, recv, to_dp, to_cell):
         pltpu.make_async_remote_copy(
@@ -260,114 +277,154 @@
     residual = to_row(gradient_sum) - roughness(cond_row, static_in[0, 0:1, :], static_in[1, 0:1, :])
     residual = jnp.where(own, residual, 0.0)
 
+    quarter = core + 2 * (cell % 2)
     for it in range(ITERS):
-        sem = 2 + 4 * it
+        sem = 2 + 5 * it
+        halo_out[it] = residual
+        for slot, (to_dp, to_cell) in enumerate(
+            (
+                (dp, above),
+                (dp, below),
+                ((dp + 1) % DP, cell),
+                ((dp + DP - 1) % DP, cell),
+            )
+        ):
+            push(
+                halo_out.at[it],
+                halo_in.at[it, slot],
+                send_sems.at[sem],
+                recv_sems.at[sem],
+                to_dp,
+                to_cell,
+            )
         column = jnp.broadcast_to(to_column(residual), (OWN, LANES))
-        plane_out[it] = residual
-        push(plane_out.at[it], plane_in.at[it, 0], send_sems.at[sem], recv_sems.at[sem], dp, above)
-        push(plane_out.at[it], plane_in.at[it, 1], send_sems.at[sem], recv_sems.at[sem], dp, below)
-        for block in range(DP):
-            image_row = jnp.sum(sens[block] * column, axis=0, keepdims=True)
-            first_out[it, block] = jnp.concatenate([image_row, residual], axis=0)
-        for step in (8, 7, 9, 6, 10, 5, 11, 4, 12, 3, 13, 2, 14, 1, 15):
-            to = (dp + step) % DP
+        for part in range(4):
+            first_out[it, part] = jnp.concatenate(
+                [
+                    jnp.sum(sens[4 * part + row] * column, axis=0, keepdims=True)
+                    for row in range(4)
+                ],
+                axis=0,
+            )
+        for slot, (to_core, to_x, to_y) in enumerate(PLANE):
+            to_dp = 2 * chip + (core + to_core) % 2
+            to_cell = (cell // 8 + to_x) % 4 * 8 + (cell + to_y) % 8
             push(
-                first_out.at[it, to],
-                first_in.at[it, dp],
+                first_out.at[it, to_dp % 2 + 2 * (to_cell % 2)],
+                first_in.at[it, slot],
                 send_sems.at[sem + 1],
                 recv_sems.at[sem + 1],
-                to,
-                cell,
-            )
-        first_in[it, dp] = first_out[it, dp]
-        await_bytes(plane_in.at[it], recv_sems.at[sem])
-        await_bytes(first_in.at[it, pl.ds(0, DP - 1)], recv_sems.at[sem + 1])
-        gathered = first_in[it]
-        partial = jnp.sum(gathered[:, 0:1, :], axis=0)
-        before = first_in[it, (dp + DP - 1) % DP][1:2, :]
-        after = first_in[it, (dp + 1) % DP][1:2, :]
-        wide = jnp.where(
-            own, residual, pltpu.roll(jnp.where(lane >= 64, before, after), 64, 1)
-        )
-        rough = roughness(wide, plane_in[it, 0], plane_in[it, 1]) + DAMPING * residual
+                to_dp,
+                to_cell,
+            )
+
+        await_bytes(halo_in.at[it], recv_sems.at[sem])
+        before, after = halo_in[it, 2], halo_in[it, 3]
+        wide = jnp.where(own, residual, pltpu.roll(jnp.where(lane >= 64, before, after), 64, 1))
+        rough = roughness(wide, halo_in[it, 0], halo_in[it, 1]) + DAMPING * residual
         scalars = jnp.where(lane == 0, lane_sum(residual * residual), 0.0)
         scalars = jnp.where(lane == 1, lane_sum(residual * rough), scalars)
         if it > 0:
             scalars = jnp.where(lane == 2, lane_sum(residual * direction_rough), scalars)
-        message = jnp.concatenate([partial, scalars], axis=0)
-        second_out[it] = message
-        for step in range(1, CELL):
+        scalar_out[it, 0] = scalars
+        for slot, (to_core, to_x, to_y) in enumerate(PLANE):
             push(
-                second_out.at[it],
-                second_in.at[it, step - 1],
+                scalar_out.at[it, 0],
+                scalar_in.at[it, slot],
+                send_sems.at[sem + 3],
+                recv_sems.at[sem + 3],
+                2 * chip + (core + to_core) % 2,
+                (cell // 8 + to_x) % 4 * 8 + (cell + to_y) % 8,
+            )
+
+        await_bytes(first_in.at[it], recv_sems.at[sem + 1])
+        partial = first_out[it, quarter] + jnp.sum(first_in[it], axis=0)
+        second_in[it, 4 * chip + quarter] = jnp.concatenate([partial, residual], axis=0)
+        for to_z, to_core, to_pair in COLUMN:
+            push(
+                second_in.at[it, 4 * chip + quarter],
+                second_in.at[it, 4 * chip + quarter],
                 send_sems.at[sem + 2],
                 recv_sems.at[sem + 2],
-                dp,
-                (cell + step) % CELL,
-            )
-        await_bytes(second_in.at[it], recv_sems.at[sem + 2])
-        message = message + jnp.sum(second_in[it], axis=0)
-        third_in[it, dp] = message
-        for step in (8, 7, 9, 6, 10, 5, 11, 4, 12, 3, 13, 2, 14, 1, 15):
+                (chip + to_z) % 8 * 2 + (core + to_core) % 2,
+                cell + to_pair * (1 - 2 * (cell % 2)),
+            )
+
+        await_bytes(scalar_in.at[it, pl.ds(0, 63)], recv_sems.at[sem + 3])
+        scalars = scalars + jnp.sum(scalar_in[it, 0:63], axis=0)
+        scalar_out[it, 1] = scalars
+        for slot, to_z in enumerate((4, 3, 5, 2, 6, 1, 7)):
             push(
-                third_in.at[it, dp],
-                third_in.at[it, dp],
-                send_sems.at[sem + 3],
-                recv_sems.at[sem + 3],
-                (dp + step) % DP,
+                scalar_out.at[it, 1],
+                scalar_in.at[it, 63 + slot],
+                send_sems.at[sem + 4],
+                recv_sems.at[sem + 4],
+                (chip + to_z) % 8 * 2 + core,
                 cell,
             )
-        await_bytes(third_in.at[it, pl.ds(0, DP - 1)], recv_sems.at[sem + 3])
-        sums = jnp.sum(third_in[it][:, 1:2, :], axis=0)
+
+        await_bytes(second_in.at[it, pl.ds(0, 31)], recv_sems.at[sem + 2])
+        quarters = [second_in[it, part] for part in range(4)]
+        for plane in range(1, 8):
+            for part in range(4):
+                quarters[part] += second_in[it, 4 * plane + part]
+        rows = [quarters[block // 4][block % 4 : block % 4 + 1] for block in range(DP)]
+        await_bytes(scalar_in.at[it, pl.ds(63, 7)], recv_sems.at[sem + 4])
+        sums = scalars + jnp.sum(scalar_in[it, 63:70], axis=0)
         norm_next = sums[:, 0:1]
         energy = sums[:, 1:2]
-        plane_rows = gathered[:, 1, :]
+        plane_rows = jnp.concatenate(
+            [
+                second_in[it, source // 2 * 4 + source % 2 + 2 * (cell % 2)][4:5]
+                for source in range(DP)
+            ],
+            axis=0,
+        )
         if it == 0:
-            predicted = [third_in[it, block][0:1, :] for block in range(DP)]
+            predicted = rows
             direction_rough = rough
-            predicted_own = message[0:1, :]
             whole = plane_rows
         else:
             ratio = norm_next / norm_now
             energy = energy + ratio * (2.0 * sums[:, 2:3] + ratio * energy_before)
-            predicted = [
-                third_in[it, block][0:1, :] + ratio * predicted[block] for block in range(DP)
-            ]
+            predicted = [rows[block] + ratio * predicted[block] for block in range(DP)]
             direction_rough = rough + ratio * direction_rough
-            predicted_own = message[0:1, :] + ratio * predicted_own
             whole = plane_rows + ratio * whole
         weighted = [setup_in[block, 4:5, :] * predicted[block] for block in range(DP)]
         square = weighted[0] * predicted[0]
         for block in range(1, DP):
             square += weighted[block] * predicted[block]
         step_length = norm_next / (energy + lane_sum(square))
-        if it == 0:
-            update = step_length * whole
-            change = step_length * predicted_own
-        else:
-            update = update + step_length * whole
-            change = change + step_length * predicted_own
         if it < ITERS - 1:
             spread = sens[0] * weighted[0]
             for block in range(1, DP):
                 spread += sens[block] * weighted[block]
             image = to_row(spread) + direction_rough
             residual = jnp.where(own, residual - step_length * image, 0.0)
+        predicted_rows = jnp.concatenate(predicted, axis=0)
+        if it == 0:
+            update = step_length * whole
+            change = step_length * predicted_rows
+        else:
+            update = update + step_length * whole
+            change = change + step_length * predicted_rows
         norm_now = norm_next
         energy_before = energy
 
     update_out[...] = update
-    change_out[...] = change
+    mine = lax.broadcasted_iota(jnp.int32, (DP, LANES), 0) == dp
+    change_out[...] = jnp.sum(jnp.where(mine, change, 0.0), axis=0, keepdims=True)
 
     await_bytes(setup_in.at[pl.ds(0, DP - 1)], send_sems.at[0])
     await_bytes(static_in, send_sems.at[1])
     await_bytes(field_in.at[pl.ds(0, DP - 1)], field_send)
     for it in range(ITERS):
-        sem = 2 + 4 * it
-        await_bytes(plane_in.at[it], send_sems.at[sem])
-        await_bytes(first_in.at[it, pl.ds(0, DP - 1)], send_sems.at[sem + 1])
-        await_bytes(second_in.at[it], send_sems.at[sem + 2])
-        await_bytes(third_in.at[it, pl.ds(0, DP - 1)], send_sems.at[sem + 3])
+        sem = 2 + 5 * it
+        await_bytes(halo_in.at[it], send_sems.at[sem])
+        await_bytes(first_in.at[it], send_sems.at[sem + 1])
+        await_bytes(second_in.at[it, pl.ds(0, 31)], send_sems.at[sem + 2])
+        await_bytes(scalar_in.at[it, pl.ds(0, 63)], send_sems.at[sem + 3])
+        await_bytes(scalar_in.at[it, pl.ds(63, 7)], send_sems.at[sem + 4])
 
 
 def per_device(configs, pole_fields, misfit, data_weight, conductivity, face_weights):
@@ -398,17 +455,17 @@
             pltpu.VMEM((DP, 8, LANES), F32),
             pltpu.VMEM((2, LANES), F32),
             pltpu.VMEM((2, 2, LANES), F32),
-            pltpu.VMEM((ITERS, DP, 2, LANES), F32),
-            pltpu.VMEM((ITERS, DP, 2, LANES), F32),
             pltpu.VMEM((ITERS, 1, LANES), F32),
+            pltpu.VMEM((ITERS, 4, 1, LANES), F32),
+            pltpu.VMEM((ITERS, 4, 4, LANES), F32),
+            pltpu.VMEM((ITERS, 63, 4, LANES), F32),
+            pltpu.VMEM((ITERS, 32, 5, LANES), F32),
             pltpu.VMEM((ITERS, 2, 1, LANES), F32),
-            pltpu.VMEM((ITERS, 2, LANES), F32),
-            pltpu.VMEM((ITERS, CELL - 1, 2, LANES), F32),
-            pltpu.VMEM((ITERS, DP, 2, LANES), F32),
+            pltpu.VMEM((ITERS, 70, 1, LANES), F32),
             pltpu.SemaphoreType.DMA,
             pltpu.SemaphoreType.DMA((DP,)),
-            pltpu.SemaphoreType.DMA((2 + 4 * ITERS,)),
-            pltpu.SemaphoreType.DMA((2 + 4 * ITERS,)),
+            pltpu.SemaphoreType.DMA((2 + 5 * ITERS,)),
+            pltpu.SemaphoreType.DMA((2 + 5 * ITERS,)),
             pltpu.SemaphoreType.DMA((6,)),
         ],
         compiler_params=pltpu.CompilerParams(

time: 91.8 us -> 86 us (0.937)
  Pallas kernels: 87.1 us -> 81.3 us
    pallas_call x1, Pallas kernels: 87.1 us -> 81.3 us  [per_device(): pl.pallas_call(kernel, name='inversion', out_shape=(jax.ShapeDtypeStruct(...]
where the time goes in v3:
time: 86 us; the launch traced here: 85.8 us
  Pallas kernels  81.3 us (95%)
  local copies, waits for them, and re-layouts  3.77 us (4%)
    pallas_call x1, Pallas kernels, per_device(): pl.pallas_call(kernel, name='inversion', out_shape=(jax.ShapeDtypeStruct(...  81.3 us
    unnamed x13, local copies, waits for them, and re-layouts  3.03 us

profile of v3, /device:TPU:1, one launch (start us, length us, event | category | flops | bytes accessed | tf_op | source)
XLA Modules:
  0.0 85.8 jit_solution(1087693882444291741)
XLA Ops:
  0.6 0.0 copy-start.2
  0.6 0.0 copy-start.3
  0.7 0.0 copy-start.4
  0.7 0.0 copy-start.5
  0.7 0.6 copy-done.2
  1.3 0.0 copy-done.3
  1.3 0.0 copy-done.4
  1.3 0.0 copy-done.5
  1.3 0.0 copy-start
  1.3 1.1 %copy-done = bf16[3,128,1024]{2,1,0:T(8,128)(2,1)S(1)} copy-done((bf16[3,128,1024]{2,1,0:T(8,128)(2,1)S(1)}, bf16[3,128,1024]{2,1,0:T(8,128)(2,1)}, u32[]{:S(2)}) %copy-start) | copy-done | bytes 786456
  2.5 0.0 copy-start.1
  2.5 0.7 copy-done.1
  3.2 81.3 %inversion.1 = (f32[16,128]{1,0:T(8,128)S(1)}, f32[1,128]{1,0:T(1,128)S(1)}) custom-call(bf16[3,128,1024]{2,1,0:T(8,128)(2,1)S(1)} %copy-done, s32[4,128]{1,0:T(4,128)S(1)} %bitcast.6, f32[1,128]{1,0:T(1,128)S(1)} %bitcast.7, f32[1,128]{1,0:T(1,128)S(1)} %bitcast.8, f32[8,128]{1,0:T(8,128)S(1)} %bitcast.5, f32[3,1024]{1,0:T(4,128)S(1)} %copy-done.1), custom_call_target="tpu_custom_call" | custom-call | tf_op jit(solution)/shard_map/inversion/pallas_call | solution.py:432
  84.5 0.1 slice.3
  84.6 0.7 reshape.22
  85.3 0.5 copy.9
Async XLA Ops:
  0.6 0.7 copy-start.2
  0.6 0.7 copy-start.3
  0.7 0.7 copy-start.4
  0.7 0.7 copy-start.5
  1.3 1.1 %copy-start = (bf16[3,128,1024]{2,1,0:T(8,128)(2,1)S(1)}, bf16[3,128,1024]{2,1,0:T(8,128)(2,1)}, u32[]{:S(2)}) copy-start(bf16[3,128,1024]{2,1,0:T(8,128)(2,1)} %fields_hbm.1) | copy-start | bytes 2359300
  2.5 0.7 copy-start.1

commit v4 on v3

--- a/solution.py
+++ b/solution.py
@@ -278,9 +278,45 @@
     residual = jnp.where(own, residual, 0.0)
 
     quarter = core + 2 * (cell % 2)
+    weights = jnp.concatenate([setup_in[block, 4:5, :] for block in range(DP)], axis=0)
+
+    def finish_step(step, held):
+        await_bytes(scalar_in.at[step, pl.ds(63, 7)], recv_sems.at[2 + 5 * step + 4])
+        sums = held["scalars"] + jnp.sum(scalar_in[step, 63:70], axis=0)
+        norm, energy = sums[:, 0:1], sums[:, 1:2]
+        predicted, rough, whole = held["image"], held["rough"], held["plane"]
+        ratio = None
+        if step > 0:
+            ratio = norm / held["norm"]
+            energy = energy + ratio * (2.0 * sums[:, 2:3] + ratio * held["energy"])
+            predicted = predicted + ratio * held["predicted"]
+            rough = rough + ratio * held["direction_rough"]
+            whole = whole + ratio * held["whole"]
+        square = jnp.sum(weights * predicted * predicted, axis=0, keepdims=True)
+        length = norm / (energy + lane_sum(square))
+        update, change = length * whole, length * predicted
+        if step > 0:
+            update, change = held["update"] + update, held["change"] + change
+        held.update(
+            norm=norm,
+            energy=energy,
+            predicted=predicted,
+            direction_rough=rough,
+            whole=whole,
+            update=update,
+            change=change,
+        )
+        return ratio, length
+
+    def along(name, value, ratio, held):
+        held[name] = value if ratio is None else value + ratio * held[name]
+        return held[name]
+
+    held = {}
+    vector = residual
     for it in range(ITERS):
         sem = 2 + 5 * it
-        halo_out[it] = residual
+        halo_out[it] = vector
         for slot, (to_dp, to_cell) in enumerate(
             (
                 (dp, above),
@@ -297,7 +333,7 @@
                 to_dp,
                 to_cell,
             )
-        column = jnp.broadcast_to(to_column(residual), (OWN, LANES))
+        column = jnp.broadcast_to(to_column(vector), (OWN, LANES))
         for part in range(4):
             first_out[it, part] = jnp.concatenate(
                 [
@@ -318,14 +354,21 @@
                 to_cell,
             )
 
+        if it > 0:
+            ratio, length = finish_step(it - 1, held)
+            residual = residual - length * along("hessian", vector, ratio, held)
+
         await_bytes(halo_in.at[it], recv_sems.at[sem])
         before, after = halo_in[it, 2], halo_in[it, 3]
-        wide = jnp.where(own, residual, pltpu.roll(jnp.where(lane >= 64, before, after), 64, 1))
-        rough = roughness(wide, halo_in[it, 0], halo_in[it, 1]) + DAMPING * residual
+        wide = jnp.where(own, vector, pltpu.roll(jnp.where(lane >= 64, before, after), 64, 1))
+        rough = roughness(wide, halo_in[it, 0], halo_in[it, 1]) + DAMPING * vector
+        if it > 0:
+            rough = held["rough"] - length * along("hessian_rough", rough, ratio, held)
+        held["rough"] = rough
         scalars = jnp.where(lane == 0, lane_sum(residual * residual), 0.0)
         scalars = jnp.where(lane == 1, lane_sum(residual * rough), scalars)
         if it > 0:
-            scalars = jnp.where(lane == 2, lane_sum(residual * direction_rough), scalars)
+            scalars = jnp.where(lane == 2, lane_sum(residual * held["direction_rough"]), scalars)
         scalar_out[it, 0] = scalars
         for slot, (to_core, to_x, to_y) in enumerate(PLANE):
             push(
@@ -363,54 +406,33 @@
                 cell,
             )
 
+        held["scalars"] = scalars
+
         await_bytes(second_in.at[it, pl.ds(0, 31)], recv_sems.at[sem + 2])
         quarters = [second_in[it, part] for part in range(4)]
         for plane in range(1, 8):
             for part in range(4):
                 quarters[part] += second_in[it, 4 * plane + part]
-        rows = [quarters[block // 4][block % 4 : block % 4 + 1] for block in range(DP)]
-        await_bytes(scalar_in.at[it, pl.ds(63, 7)], recv_sems.at[sem + 4])
-        sums = scalars + jnp.sum(scalar_in[it, 63:70], axis=0)
-        norm_next = sums[:, 0:1]
-        energy = sums[:, 1:2]
-        plane_rows = jnp.concatenate(
+        image = jnp.concatenate([rows[0:4] for rows in quarters], axis=0)
+        if it > 0:
+            image = held["image"] - length * along("hessian_image", image, ratio, held)
+        held["image"] = image
+        if it < ITERS - 1:
+            weighted = weights * image
+            spread = sens[0] * weighted[0:1]
+            for block in range(1, DP):
+                spread += sens[block] * weighted[block : block + 1]
+            vector = jnp.where(own, to_row(spread) + rough, 0.0)
+        held["plane"] = jnp.concatenate(
             [
                 second_in[it, source // 2 * 4 + source % 2 + 2 * (cell % 2)][4:5]
                 for source in range(DP)
             ],
             axis=0,
         )
-        if it == 0:
-            predicted = rows
-            direction_rough = rough
-            whole = plane_rows
-        else:
-            ratio = norm_next / norm_now
-            energy = energy + ratio * (2.0 * sums[:, 2:3] + ratio * energy_before)
-            predicted = [rows[block] + ratio * predicted[block] for block in range(DP)]
-            direction_rough = rough + ratio * direction_rough
-            whole = plane_rows + ratio * whole
-        weighted = [setup_in[block, 4:5, :] * predicted[block] for block in range(DP)]
-        square = weighted[0] * predicted[0]
-        for block in range(1, DP):
-            square += weighted[block] * predicted[block]
-        step_length = norm_next / (energy + lane_sum(square))
-        if it < ITERS - 1:
-            spread = sens[0] * weighted[0]
-            for block in range(1, DP):
-                spread += sens[block] * weighted[block]
-            image = to_row(spread) + direction_rough
-            residual = jnp.where(own, residual - step_length * image, 0.0)
-        predicted_rows = jnp.concatenate(predicted, axis=0)
-        if it == 0:
-            update = step_length * whole
-            change = step_length * predicted_rows
-        else:
-            update = update + step_length * whole
-            change = change + step_length * predicted_rows
-        norm_now = norm_next
-        energy_before = energy
-
+
+    finish_step(ITERS - 1, held)
+    update, change = held["update"], held["change"]
     update_out[...] = update
     mine = lax.broadcasted_iota(jnp.int32, (DP, LANES), 0) == dp
     change_out[...] = jnp.sum(jnp.where(mine, change, 0.0), axis=0, keepdims=True)

time: 86 us -> 82.5 us (0.959)
  Pallas kernels: 81.3 us -> 77.8 us
    pallas_call x1, Pallas kernels: 81.3 us -> 77.8 us  [per_device(): pl.pallas_call(kernel, name='inversion', out_shape=(jax.ShapeDtypeStruct(...]
where the time goes in v4:
time: 82.5 us; the launch traced here: 82.2 us
  Pallas kernels  77.8 us (94%)
  local copies, waits for them, and re-layouts  3.77 us (5%)
    pallas_call x1, Pallas kernels, per_device(): pl.pallas_call(kernel, name='inversion', out_shape=(jax.ShapeDtypeStruct(...  77.8 us
    unnamed x13, local copies, waits for them, and re-layouts  3.03 us

profile of v4, /device:TPU:1, one launch (start us, length us, event | category | flops | bytes accessed | tf_op | source)
XLA Modules:
  0.0 82.2 jit_solution(12124751313741597462)
XLA Ops:
  0.6 0.0 copy-start.2
  0.6 0.0 copy-start.3
  0.7 0.0 copy-start.4
  0.7 0.0 copy-start.5
  0.7 0.6 copy-done.2
  1.3 0.0 copy-done.3
  1.3 0.0 copy-done.4
  1.3 0.0 copy-done.5
  1.3 0.0 copy-start
  1.3 1.1 %copy-done = bf16[3,128,1024]{2,1,0:T(8,128)(2,1)S(1)} copy-done((bf16[3,128,1024]{2,1,0:T(8,128)(2,1)S(1)}, bf16[3,128,1024]{2,1,0:T(8,128)(2,1)}, u32[]{:S(2)}) %copy-start) | copy-done | bytes 786456
  2.5 0.0 copy-start.1
  2.5 0.7 copy-done.1
  3.2 77.8 %inversion.1 = (f32[16,128]{1,0:T(8,128)S(1)}, f32[1,128]{1,0:T(1,128)S(1)}) custom-call(bf16[3,128,1024]{2,1,0:T(8,128)(2,1)S(1)} %copy-done, s32[4,128]{1,0:T(4,128)S(1)} %bitcast.6, f32[1,128]{1,0:T(1,128)S(1)} %bitcast.7, f32[1,128]{1,0:T(1,128)S(1)} %bitcast.8, f32[8,128]{1,0:T(8,128)S(1)} %bitcast.5, f32[3,1024]{1,0:T(4,128)S(1)} %copy-done.1), custom_call_target="tpu_custom_call" | custom-call | tf_op jit(solution)/shard_map/inversion/pallas_call | solution.py:454
  81.0 0.1 slice.3
  81.0 0.7 reshape.22
  81.7 0.5 copy.9
Async XLA Ops:
  0.6 0.7 copy-start.2
  0.6 0.7 copy-start.3
  0.7 0.7 copy-start.4
  0.7 0.7 copy-start.5
  1.3 1.1 %copy-start = (bf16[3,128,1024]{2,1,0:T(8,128)(2,1)S(1)}, bf16[3,128,1024]{2,1,0:T(8,128)(2,1)}, u32[]{:S(2)}) copy-start(bf16[3,128,1024]{2,1,0:T(8,128)(2,1)} %fields_hbm.1) | copy-start | bytes 2359300
  2.5 0.7 copy-start.1

commit v5 on v4

--- a/solution.py
+++ b/solution.py
@@ -423,13 +423,13 @@
             for block in range(1, DP):
                 spread += sens[block] * weighted[block : block + 1]
             vector = jnp.where(own, to_row(spread) + rough, 0.0)
-        held["plane"] = jnp.concatenate(
-            [
-                second_in[it, source // 2 * 4 + source % 2 + 2 * (cell % 2)][4:5]
-                for source in range(DP)
-            ],
-            axis=0,
-        )
+        mine = [
+            second_in[it, source // 2 * 4 + source % 2 + 2 * (cell % 2)][4:5]
+            for source in range(DP)
+        ]
+        left = pltpu.roll(jnp.concatenate(mine[0::2], axis=0), 96, 1)
+        right = pltpu.roll(jnp.concatenate(mine[1::2], axis=0), 32, 1)
+        held["plane"] = jnp.where(lane < 64, left, right)
 
     finish_step(ITERS - 1, held)
     update, change = held["update"], held["change"]
@@ -455,7 +455,7 @@
         kernel,
         name="inversion",
         out_shape=(
-            jax.ShapeDtypeStruct((DP, LANES), F32),
+            jax.ShapeDtypeStruct((8, LANES), F32),
             jax.ShapeDtypeStruct((1, LANES), F32),
         ),
         in_specs=[pl.BlockSpec(memory_space=pltpu.HBM)] * 6,
@@ -491,7 +491,7 @@
             pltpu.SemaphoreType.DMA((6,)),
         ],
         compiler_params=pltpu.CompilerParams(
-            collective_id=0, has_side_effects=True, vmem_limit_bytes=40 * 1024 * 1024
+            collective_id=0, has_side_effects=True, vmem_limit_bytes=60 * 1024 * 1024
         ),
     )(
         pole_fields,
@@ -501,7 +501,7 @@
         conductivity.reshape(8, LANES),
         face_weights,
     )
-    return update[:, 32:96].reshape(-1), change.reshape(-1)
+    return update.reshape(-1), change.reshape(-1)
 
 
 def solution(mesh):

time: 82.5 us -> 80.5 us (0.976)
  local copies, waits for them, and re-layouts: 3.77 us -> 1.82 us
    unnamed x13 -> x6, local copies, waits for them, and re-layouts: 3.03 us -> 1.82 us
where the time goes in v5:
time: 80.5 us; the launch traced here: 80.3 us
  Pallas kernels  77.8 us (97%)
  local copies, waits for them, and re-layouts  1.82 us (2%)
    pallas_call x1, Pallas kernels, per_device(): pl.pallas_call(kernel, name='inversion', out_shape=(jax.ShapeDtypeStruct(...  77.8 us
    unnamed x6, local copies, waits for them, and re-layouts  1.82 us

profile of v5, /device:TPU:1, one launch (start us, length us, event | category | flops | bytes accessed | tf_op | source)
XLA Modules:
  0.0 80.3 jit_solution(16354084656962229457)
XLA Ops:
  0.6 77.8 %inversion.1 = (f32[8,128]{1,0:T(8,128)}, f32[1,128]{1,0:T(1,128)}) custom-call(bf16[3,128,1024]{2,1,0:T(8,128)(2,1)} %fields_hbm.1, s32[4,128]{1,0:T(4,128)} %bitcast.8, f32[1,128]{1,0:T(1,128)} %bitcast.9, f32[1,128]{1,0:T(1,128)} %bitcast.10, f32[8,128]{1,0:T(8,128)} %bitcast.6, f32[3,1024]{1,0:T(4,128)} %faces_hbm.1), custom_call_target="tpu_custom_call" | custom-call | tf_op jit(solution)/shard_map/inversion/pallas_call | solution.py:454
  78.4 0.0 copy-start
  78.5 0.7 copy-done
  79.1 0.0 copy-start.1
  79.1 0.6 copy.10
  79.7 0.0 copy-done.1
  79.8 0.5 copy.11
Async XLA Ops:
  78.4 0.7 copy-start
  79.1 0.6 copy-start.1

commit v6 on v5

--- a/solution.py
+++ b/solution.py
@@ -447,6 +447,11 @@
         await_bytes(second_in.at[it, pl.ds(0, 31)], send_sems.at[sem + 2])
         await_bytes(scalar_in.at[it, pl.ds(0, 63)], send_sems.at[sem + 3])
         await_bytes(scalar_in.at[it, pl.ds(63, 7)], send_sems.at[sem + 4])
+
+
+def hand_on_kernel(update, change, update_out, change_out):
+    update_out[...] = update[...]
+    change_out[...] = change[...]
 
 
 def per_device(configs, pole_fields, misfit, data_weight, conductivity, face_weights):
@@ -501,6 +506,18 @@
         conductivity.reshape(8, LANES),
         face_weights,
     )
+    hand_on = pl.pallas_call(
+        hand_on_kernel,
+        name="results",
+        out_shape=(
+            jax.ShapeDtypeStruct((8, LANES), F32),
+            jax.ShapeDtypeStruct((1, LANES), F32),
+        ),
+        in_specs=[pl.BlockSpec(memory_space=pltpu.VMEM)] * 2,
+        out_specs=(pl.BlockSpec(memory_space=pltpu.VMEM),) * 2,
+        scratch_shapes=[],
+    )
+    update, change = hand_on(update, change)
     return update.reshape(-1), change.reshape(-1)
 
 

time: 80.5 us -> 79.9 us (level)
  local copies, waits for them, and re-layouts: 1.82 us -> 0 us
  Pallas kernels: 77.8 us -> 79.1 us
    unnamed x6 -> x0, local copies, waits for them, and re-layouts: 1.82 us -> none
    pallas_call x0 -> x1, Pallas kernels: none -> 1.27 us  [per_device(): update, change = hand_on(update, change)]
where the time goes in v6:
time: 79.9 us; the launch traced here: 79.7 us
  Pallas kernels  79.1 us (99%)
    pallas_call x1, Pallas kernels, per_device(): pl.pallas_call(kernel, name='inversion', out_shape=(jax.ShapeDtypeStruct(...  77.8 us

profile of v6, /device:TPU:1, one launch (start us, length us, event | category | flops | bytes accessed | tf_op | source)
XLA Modules:
  0.0 79.7 jit_solution(10421012345850843569)
XLA Ops:
  0.6 77.8 %inversion.1 = (f32[8,128]{1,0:T(8,128)}, f32[1,128]{1,0:T(1,128)}) custom-call(bf16[3,128,1024]{2,1,0:T(8,128)(2,1)} %fields_hbm.1, s32[4,128]{1,0:T(4,128)} %bitcast.7, f32[1,128]{1,0:T(1,128)} %bitcast.8, f32[1,128]{1,0:T(1,128)} %bitcast.9, f32[8,128]{1,0:T(8,128)} %bitcast.6, f32[3,1024]{1,0:T(4,128)} %faces_hbm.1), custom_call_target="tpu_custom_call" | custom-call | tf_op jit(solution)/shard_map/inversion/pallas_call | solution.py:459
  78.4 1.3 %results.1 = (f32[8,128]{1,0:T(8,128)}, f32[1,128]{1,0:T(1,128)}) custom-call(f32[8,128]{1,0:T(8,128)} %get-tuple-element.6.update, f32[1,128]{1,0:T(1,128)} %get-tuple-element.7.change), custom_call_target="tpu_custom_call" | custom-call | tf_op jit(solution)/shard_map/results/pallas_call | solution.py:520
